TPU v7x, 512 devices: a whole 4x4x16 slice. The times are simulated.
512 devices in a mesh: tile: 128 (over y_lo, x, z), dir: 4 (over y_hi, core).
Axes of the slice: x: 4, y: 4 (y_hi: 2, y_lo: 2; y = y_hi * 2 + y_lo), z: 16, core: 2. Of those that a mesh axis runs over, the one named last changes fastest.
Arguments:
- layers: bfloat16 [4, 16384, 2048], P('dir', 'tile'), may hold values from -6 to 6
- offsets: int32 [4, 4, 2], replicated, may hold values from 0 to 8191, as said below
- subap_valid: int32 [128, 16], P('tile'), may hold values from 0 to 1, as said below
- defocus: float32 [3], replicated, may hold values from -0.08 to 0.08
- weights: float32 [3], replicated, may hold values from 0.25 to 1
Outputs:
- spots: bfloat16 [4, 128, 128, 2048], P('dir', 'tile')
Inputs may be any that keep to these rules, and one draw needn't show every extreme that they name: offsets[d, l, 0] < 1024 and offsets[d, l, 1] < 8192; both bounds minus one are taken by some pair in every draw. `subap_valid`: the part of an annulus of lit subapertures that falls in the strip, with a few dead ones.
All inputs are finite; a program needn't handle non-finite values.
Results may differ from a plain program's by a relative error of at most 0.0055.
Values may be sent and summed in bfloat16 or wider, within the bound.
No kernel may reach another device: no remote copies, remote signals or barrier semaphores. Data moves between devices by JAX's collectives and lax.ppermute only.
A program may use at most 64 MiB of HBM per device.

v0:
```python
import math
import jax
import jax.numpy as jnp
from jax import lax
from jax.sharding import PartitionSpec as P

SUBPIX = 128
SPOT = 128
SUBX = 16
SLICES = 3
REACH = 2
QUANT = 4
OVER = 2
PCOLS = 2048


def shifted(value, axis, by):
    count = lax.axis_size(axis)
    return lax.ppermute(value, axis, [(i, (i + by) % count) for i in range(count)])


def tables():
    frequency = jnp.arange(SPOT, dtype=jnp.float32) - SPOT // 2
    position = jnp.arange(SUBPIX, dtype=jnp.float32) - (SUBPIX - 1) / 2.0
    phase_angle = -2.0 * math.pi / (OVER * SUBPIX) * frequency[:, None] * position[None, :]
    factor = 1.0 / math.sqrt(SUBPIX)
    real_part = jnp.cos(phase_angle) * factor
    imag_part = jnp.sin(phase_angle) * factor
    left_table = jnp.concatenate(
        [jnp.concatenate([real_part, -imag_part], 1), jnp.concatenate([imag_part, real_part], 1)], 0
    ).astype(jnp.bfloat16)
    right_table = jnp.concatenate(
        [
            jnp.concatenate([real_part.T, imag_part.T], 1),
            jnp.concatenate([-imag_part.T, real_part.T], 1),
        ],
        0,
    ).astype(jnp.bfloat16)
    return (left_table, right_table)


def interpolate(window, offset_pair):
    col_steps = offset_pair[1] // QUANT
    col_frac = (offset_pair[1] % QUANT).astype(jnp.float32) / QUANT
    row_frac = (offset_pair[0] % QUANT).astype(jnp.float32) / QUANT
    col_first = jnp.roll(window, -col_steps, axis=1)
    col_second = jnp.roll(window, -(col_steps + 1), axis=1)
    across = (1.0 - col_frac) * col_first + col_frac * col_second
    return ((1.0 - row_frac) * across[:-1] + row_frac * across[1:]).astype(jnp.bfloat16)


def spots_row(pupil_phase, first_row, total_rows, defocus, weights, valid_row):
    left_table, right_table = tables()
    row_position = (
        (first_row + jnp.arange(SUBPIX, dtype=jnp.int32)).astype(jnp.float32)
        - (total_rows - 1) / 2.0
    ) / SUBPIX
    col_position = (jnp.arange(PCOLS, dtype=jnp.float32) - (PCOLS - 1) / 2.0) / SUBPIX
    radius = row_position[:, None] ** 2 + col_position[None, :] ** 2
    spot_sum = jnp.zeros((SPOT * SUBX, SPOT), jnp.float32)
    for altitude in range(SLICES):
        phase_angle = pupil_phase + defocus[altitude] * radius
        pupil_field = jnp.concatenate([jnp.cos(phase_angle), jnp.sin(phase_angle)], 0).astype(
            jnp.bfloat16
        )
        focal_plane = jnp.dot(left_table, pupil_field, preferred_element_type=jnp.float32).astype(
            jnp.bfloat16
        )
        blocks = jnp.concatenate(
            [
                focal_plane[:SPOT].reshape(SPOT * SUBX, SUBPIX),
                focal_plane[SPOT:].reshape(SPOT * SUBX, SUBPIX),
            ],
            1,
        )
        spot_field = jnp.dot(blocks, right_table, preferred_element_type=jnp.float32)
        spot_sum = spot_sum + weights[altitude] * (
            spot_field[:, :SPOT] ** 2 + spot_field[:, SPOT:] ** 2
        )
    scaled = spot_sum / jnp.sum(weights)
    masked = scaled.reshape(SPOT, SUBX, SPOT) * valid_row.astype(jnp.float32)[None, :, None]
    return masked.reshape(SPOT, SUBX * SPOT).astype(jnp.bfloat16)


def extend(block):
    pieces = [block]
    for distance in range(1, REACH + 1):
        pieces.append(shifted(block, "tile", -distance))
    return jnp.concatenate(pieces, 1)


def shifted_term(extended, offset_pair):
    window = lax.dynamic_slice_in_dim(extended, offset_pair[0] // QUANT, SUBPIX + 1, 0).astype(
        jnp.float32
    )
    return interpolate(window, offset_pair)


def shards(layers, offsets, subap_valid, defocus, weights):
    own_dir = lax.axis_index("dir")
    tile_index = lax.axis_index("tile")
    total_rows = lax.axis_size("tile") * SUBPIX
    pupil_phase = jnp.zeros((SUBPIX, PCOLS), jnp.float32)
    stacked = lax.all_gather(layers, "dir", axis=0, tiled=True)
    extended = extend(stacked)
    offset_pairs = lax.dynamic_index_in_dim(offsets, own_dir, 0, keepdims=False)
    for layer_index in range(stacked.shape[0]):
        pupil_phase = pupil_phase + shifted_term(
            extended[layer_index], offset_pairs[layer_index]
        ).astype(jnp.float32)
    spots = spots_row(
        pupil_phase, tile_index * SUBPIX, total_rows, defocus, weights, subap_valid[0]
    )
    return spots[None, None]


def solution(mesh):
    placed = (P("dir", "tile", None), P(), P("tile", None), P(), P())
    return jax.shard_map(
        shards, mesh=mesh, in_specs=placed, out_specs=P("dir", "tile", None, None), check_vma=False
    )
```

profile of v0, /device:TPU:1, one launch (start us, length us, event | category | flops | bytes accessed | tf_op | source)
XLA Modules:
  0.0 236.5 jit_solution(6538307953497980572)
XLA Ops:
  6.5 0.0 copy-start
  6.5 0.0 all-gather.2.cloned.1.call-start
  6.5 0.7 all-gather.2.cloned.1.call-update
  7.3 42.3 %all-gather.2.cloned.1.call-done = bf16[4,128,2048]{2,1,0:T(8,128)(2,1)} async-done(((bf16[1,128,2048]{2,1,0:T(8,128)(2,1)}), bf16[4,128,2048]{2,1,0:T(8,128)(2,1)}) %all-gather.2.cloned.1.call-update) | async-done | bytes 2097168 | tf_op jit(solution)/shard_map/all_gather | solution.py:104
  49.5 7.8 %collective-permute-start = (bf16[4,128,2048]{2,1,0:T(8,128)(2,1)}, bf16[4,128,2048]{2,1,0:T(8,128)(2,1)}, u32[]{:S(2)}, u32[]{:S(2)}) collective-permute-start(bf16[4,128,2048]{2,1,0:T(8,128)(2,1)} %all-gather.2.cloned.1.call-done), channel_id=1, source_target_pairs={{0,508},{4,0},{8,4},{12,8},{16,12},{20,16},{24,20},{28,24},{32,28}... | collective-permute-start | bytes 6291464 | tf_op jit(solution)/shard_map/ppermute | solution.py:19
  57.4 3.8 %collective-permute-start.1 = (bf16[4,128,2048]{2,1,0:T(8,128)(2,1)}, bf16[4,128,2048]{2,1,0:T(8,128)(2,1)S(1)}, u32[]{:S(2)}, u32[]{:S(2)}) collective-permute-start(bf16[4,128,2048]{2,1,0:T(8,128)(2,1)} %all-gather.2.cloned.1.call-done), channel_id=1, source_target_pairs={{0,504},{4,508},{8,0},{12,4},{16,8},{20,12},{24,16},{28,20},{32,24... | collective-permute-start | bytes 6291464 | tf_op jit(solution)/shard_map/ppermute | solution.py:19
  61.2 0.0 copy-done
  61.2 0.7 fusion.83
  83.2 1.3 reduce_sum.9
  84.5 1.4 fusion.84
  85.9 1.4 fusion.85
  87.4 0.7 convert_bitcast_fusion
  88.0 0.1 broadcast_bitcast_fusion
  88.1 0.6 fusion.71
  88.6 1.7 constant_dynamic-update-slice_fusion.2
  90.4 18.5 %collective-permute-done = bf16[4,128,2048]{2,1,0:T(8,128)(2,1)} collective-permute-done((bf16[4,128,2048]{2,1,0:T(8,128)(2,1)}, bf16[4,128,2048]{2,1,0:T(8,128)(2,1)}, u32[]{:S(2)}, u32[]{:S(2)}) %collective-permute-start) | collective-permute-done | bytes 2097184 | tf_op jit(solution)/shard_map/ppermute | solution.py:19
  108.9 1.7 constant_dynamic-update-slice_fusion.1
  110.6 81.7 %collective-permute-done.1 = bf16[4,128,2048]{2,1,0:T(8,128)(2,1)S(1)} collective-permute-done((bf16[4,128,2048]{2,1,0:T(8,128)(2,1)}, bf16[4,128,2048]{2,1,0:T(8,128)(2,1)S(1)}, u32[]{:S(2)}, u32[]{:S(2)}) %collective-permute-start.1) | collective-permute-done | bytes 2097184 | tf_op jit(solution)/shard_map/ppermute | solution.py:19
  192.3 0.1 constant_dynamic-update-slice_fusion
  192.4 1.0 fusion.79
  193.4 0.3 bitcast_convert_fusion.2
  193.7 1.2 fusion.17
  195.0 1.2 fusion.12
  196.2 0.3 bitcast_convert_fusion
  196.6 1.2 fusion.7
  197.8 1.2 fusion.2
  199.0 5.3 %cosine_convert_fusion.2 = (bf16[128,2048]{1,0:T(8,128)(2,1)S(1)}, f32[128,2048]{1,0:T(8,128)S(1)}) fusion(f32[2048]{0:T(1024)S(1)} %multiply_multiply_fusion, f32[128]{0:T(128)S(1)} %multiply_multiply_fusion.1, f32[]{:T(128)} %bitcast.17, f32[129,2048]{1,0:T(8,128)S(1)} %fusion.2, f32[]{:T(128)S(6)} %div.123, f32[]{:T(128)S(6)} %sub.110, ...), kind=kLoop, calls=%fused_computation.103 | loop fusion | flops 7077888 | bytes 9970212 | tf_op jit(solution)/shard_map/convert.14
  204.4 13.9 %sine_convert_fusion.2 = (bf16[128,2048]{1,0:T(8,128)(2,1)S(1)}, bf16[128,2048]{1,0:T(8,128)(2,1)S(1)}, bf16[128,2048]{1,0:T(8,128)(2,1)S(1)}, bf16[128,2048]{1,0:T(8,128)(2,1)}, bf16[128,2048]{1,0:T(8,128)(2,1)S(1)}) fusion(f32[128,2048]{1,0:T(8,128)S(1)} %get-tuple-element.7, f32[2048]{0:T(1024)S(1)} %multiply_multiply_fusion, ...), kind=kLoop, calls=%fused_computation.102 | loop fusion | flops 3145728 | bytes 3678732 | tf_op jit(solution)/shard_map/convert.15
  218.3 0.4 convolution_convert_fusion.2
  218.7 0.1 fusion.80
  218.8 0.2 reshape.129
  219.0 0.2 reshape.130
  219.3 0.4 convolution_convert_fusion.1
  219.7 0.1 fusion.81
  219.8 0.2 reshape.131
  220.1 0.2 reshape.132
  220.3 1.5 convolution_convert_fusion
  221.8 0.9 fusion.82
  222.7 0.2 reshape.133
  223.0 1.3 reshape.134
  224.3 0.4 fusion.43
  224.7 0.4 fusion.50
  225.1 0.4 fusion.57
  225.5 3.1 %fusion.26 = f32[2048,128]{1,0:T(8,128)S(1)} fusion(f32[2048,256]{1,0:T(8,128)S(1)} %fusion.57, f32[2048,256]{1,0:T(8,128)S(1)} %fusion.50, f32[2048,256]{1,0:T(8,128)S(1)} %fusion.43, f32[]{:T(128)} %reduce_sum.9, f32[]{:T(128)} %bitcast.20, f32[]{:T(128)} %bitcast.18, f32[]{:T(128)} %bitcast), kind=kLoop, calls=%fused_computation.49 | loop fusion | flops 3932160 | bytes 7340048 | tf_op jit(solution)/shard_map/div | solution.py:80
  228.6 0.2 reshape.135
  228.8 0.9 multiply_convert_fusion
  (4 shorter events, 0.0 us)
Async XLA Ops:
  6.5 54.6 %copy-start = (s32[4,4,2]{1,2,0:T(2,128)S(1)}, s32[4,4,2]{1,2,0:T(2,128)}, u32[]{:S(2)}) copy-start(s32[4,4,2]{1,2,0:T(2,128)} %param.8) | copy-start | bytes 388
  6.5 43.0 %all-gather.2.cloned.1.call-start = ((), (), s32[]{:S(2)}) async-start(), calls=%async_computation | async-start | bytes 2621440 | tf_op jit(solution)/shard_map/all_gather | solution.py:104
  49.5 59.4 %collective-permute-start = (bf16[4,128,2048]{2,1,0:T(8,128)(2,1)}, bf16[4,128,2048]{2,1,0:T(8,128)(2,1)}, u32[]{:S(2)}, u32[]{:S(2)}) collective-permute-start(bf16[4,128,2048]{2,1,0:T(8,128)(2,1)} %all-gather.2.cloned.1.call-done), channel_id=1, source_target_pairs={{0,508},{4,0},{8,4},{12,8},{16,12},{20,16},{24,20},{28,24},{32,28}... | collective-permute-start | bytes 6291464 | tf_op jit(solution)/shard_map/ppermute | solution.py:19
  57.4 134.9 %collective-permute-start.1 = (bf16[4,128,2048]{2,1,0:T(8,128)(2,1)}, bf16[4,128,2048]{2,1,0:T(8,128)(2,1)S(1)}, u32[]{:S(2)}, u32[]{:S(2)}) collective-permute-start(bf16[4,128,2048]{2,1,0:T(8,128)(2,1)} %all-gather.2.cloned.1.call-done), channel_id=1, source_target_pairs={{0,504},{4,508},{8,0},{12,4},{16,8},{20,12},{24,16},{28,20},{32,24... | collective-permute-start | bytes 6291464 | tf_op jit(solution)/shard_map/ppermute | solution.py:19
Sparse Core Ops, SparseCore 0:
  9.5 40.0 all-gather.1
where the time goes:
time: 237 us
  waiting for transfers between devices  143 us (60%)
  between operations  34.9 us (15%)
  other arithmetic  31.4 us (13%)
  local copies, waits for them, and re-layouts  11.9 us (5%)
  starting transfers between devices  11.6 us (5%)
  matrix products  3.66 us (2%)
    ppermute x2, waiting for transfers between devices, shifted(): lax.ppermute(value, axis, [(i, (i + by) % count) for i in range(count)])  100 us
    all_gather x1, waiting for transfers between devices, shards(): stacked = lax.all_gather(layers, 'dir', axis=0, tiled=True)  42.3 us
    another operation x3, other arithmetic  19.8 us
    ppermute x2, starting transfers between devices, shifted(): lax.ppermute(value, axis, [(i, (i + by) % count) for i in range(count)])  11.6 us
    add x4, other arithmetic, interpolate(): across = (1.0 - col_frac) * col_first + col_frac * col_second  4.96 us
  transfers between devices with their start and end apart: 3, of which 3 were waited for; matrix products, arithmetic and copies ran while one was open for 4% of the time, Pallas kernels for 0%

commit v1 on v0

--- a/solution.py
+++ b/solution.py
@@ -12,6 +12,11 @@
 QUANT = 4
 OVER = 2
 PCOLS = 2048
+
+
+def swapped_in(array, name, d):
+    sent = jnp.stack([array] * lax.axis_size(name))
+    return jnp.concatenate(lax.all_to_all(sent, name, 0, 0), axis=d)
 
 
 def shifted(value, axis, by):
@@ -101,7 +106,7 @@
     tile_index = lax.axis_index("tile")
     total_rows = lax.axis_size("tile") * SUBPIX
     pupil_phase = jnp.zeros((SUBPIX, PCOLS), jnp.float32)
-    stacked = lax.all_gather(layers, "dir", axis=0, tiled=True)
+    stacked = swapped_in(layers, "dir", 0)
     extended = extend(stacked)
     offset_pairs = lax.dynamic_index_in_dim(offsets, own_dir, 0, keepdims=False)
     for layer_index in range(stacked.shape[0]):

time: 237 us -> 222 us (0.937)
  waiting for transfers between devices: 143 us -> 106 us
  blocking collectives: 0 us -> 35.6 us
  between operations: 34.9 us -> 21.5 us
  local copies, waits for them, and re-layouts: 11.9 us -> 8.04 us
    all_gather x1 -> x0, waiting for transfers between devices: 42.3 us -> none  [shards(): stacked = lax.all_gather(layers, 'dir', axis=0, tiled=True)]
    all_to_all x0 -> x1, blocking collectives: none -> 35.6 us  [swapped_in(): return jnp.concatenate(lax.all_to_all(sent, name, 0, 0), axis=d)]
    ppermute x2, waiting for transfers between devices: 100 us -> 106 us  [shifted(): lax.ppermute(value, axis, [(i, (i + by) % count) for i in range(count)])]
    unnamed x4 -> x8, local copies, waits for them, and re-layouts: 3.46 us -> 0.02 us
    concatenate x0 -> x1, other arithmetic: none -> 3.18 us  [extend(): return jnp.concatenate(pieces, 1)]
  transfers between devices with their start and end apart: 3 -> 2, of which waited for: 3 -> 2; matrix products, arithmetic and copies ran while one was open for 4% -> 1% of each run, Pallas kernels for 0% -> 0%
where the time goes in v1:
time: 222 us; the launch traced here: 221 us
  waiting for transfers between devices  106 us (48%)
  blocking collectives  35.6 us (16%)
  other arithmetic  33 us (15%)
  between operations  21.5 us (10%)
  starting transfers between devices  12.9 us (6%)
  local copies, waits for them, and re-layouts  8.04 us (4%)
  matrix products  3.68 us (2%)
    ppermute x2, waiting for transfers between devices, shifted(): lax.ppermute(value, axis, [(i, (i + by) % count) for i in range(count)])  106 us
    all_to_all x1, blocking collectives, swapped_in(): return jnp.concatenate(lax.all_to_all(sent, name, 0, 0), axis=d)  35.6 us
    another operation x3, other arithmetic  19.6 us
    ppermute x2, starting transfers between devices, shifted(): lax.ppermute(value, axis, [(i, (i + by) % count) for i in range(count)])  12.9 us
    add x4, other arithmetic, interpolate(): across = (1.0 - col_frac) * col_first + col_frac * col_second  4.96 us
  transfers between devices with their start and end apart: 2, of which 2 were waited for; matrix products, arithmetic and copies ran while one was open for 1% of the time, Pallas kernels for 0%

profile of v1, /device:TPU:1, one launch (start us, length us, event | category | flops | bytes accessed | tf_op | source)
XLA Modules:
  0.0 220.9 jit_solution(1930579109794202567)
XLA Ops:
  0.0 0.0 copy-start
  0.0 1.3 stack.2
  1.3 0.0 copy-start.1
  1.3 0.0 copy-start.2
  1.3 0.0 copy-start.3
  1.3 35.6 %all_to_all.5 = bf16[4,1,128,2048]{3,2,1,0:T(8,128)(2,1)S(1)} all-to-all(bf16[4,1,128,2048]{3,2,1,0:T(8,128)(2,1)S(1)} %stack.2), channel_id=1, replica_groups=mesh['tile'=128,'dir'=4] {'dir'}, dimensions={0} | all-to-all | bytes 4194304 | tf_op jit(solution)/shard_map/all_to_all | solution.py:19
  37.0 9.8 %collective-permute-start = (bf16[4,128,2048]{2,1,0:T(8,128)(2,1)S(1)}, bf16[4,128,2048]{2,1,0:T(8,128)(2,1)}, u32[]{:S(2)}, u32[]{:S(2)}) collective-permute-start(bf16[4,128,2048]{2,1,0:T(8,128)(2,1)S(1)} %bitcast.32), channel_id=1, source_target_pairs={{0,508},{4,0},{8,4},{12,8},{16,12},{20,16},{24,20},{28,24},{32,28}... | collective-permute-start | bytes 6291464 | tf_op jit(solution)/shard_map/ppermute | solution.py:24
  46.8 3.1 %collective-permute-start.1 = (bf16[4,128,2048]{2,1,0:T(8,128)(2,1)S(1)}, bf16[4,128,2048]{2,1,0:T(8,128)(2,1)}, u32[]{:S(2)}, u32[]{:S(2)}) collective-permute-start(bf16[4,128,2048]{2,1,0:T(8,128)(2,1)S(1)} %bitcast.33), channel_id=1, source_target_pairs={{0,504},{4,508},{8,0},{12,4},{16,8},{20,12},{24,16},{28,20},{32,24... | collective-permute-start | bytes 6291464 | tf_op jit(solution)/shard_map/ppermute | solution.py:24
  49.9 0.0 copy-done
  50.0 0.7 fusion.83
  71.9 0.0 copy-done.1
  71.9 0.7 reduce_sum.9
  72.6 0.6 fusion.84
  73.2 0.0 copy-done.2
  73.2 0.7 fusion.85
  73.9 0.0 copy-done.3
  73.9 0.1 broadcast_bitcast_fusion
  74.0 0.6 fusion.71
  74.6 20.2 %collective-permute-done = bf16[4,128,2048]{2,1,0:T(8,128)(2,1)} collective-permute-done((bf16[4,128,2048]{2,1,0:T(8,128)(2,1)S(1)}, bf16[4,128,2048]{2,1,0:T(8,128)(2,1)}, u32[]{:S(2)}, u32[]{:S(2)}) %collective-permute-start) | collective-permute-done | bytes 2097184 | tf_op jit(solution)/shard_map/ppermute | solution.py:24
  94.8 85.8 %collective-permute-done.1 = bf16[4,128,2048]{2,1,0:T(8,128)(2,1)} collective-permute-done((bf16[4,128,2048]{2,1,0:T(8,128)(2,1)S(1)}, bf16[4,128,2048]{2,1,0:T(8,128)(2,1)}, u32[]{:S(2)}, u32[]{:S(2)}) %collective-permute-start.1) | collective-permute-done | bytes 2097184 | tf_op jit(solution)/shard_map/ppermute | solution.py:24
  180.6 3.2 %pad_maximum_fusion = bf16[4,384,2048]{2,1,0:T(8,128)(2,1)S(1)} fusion(bf16[4,128,2048]{2,1,0:T(8,128)(2,1)} %collective-permute-done.1, bf16[4,128,2048]{2,1,0:T(8,128)(2,1)} %collective-permute-done, bf16[4,128,2048]{2,1,0:T(8,128)(2,1)S(1)} %bitcast.34), kind=kLoop, calls=%fused_computation | loop fusion | flops 18874368 | bytes 12582912 | tf_op jit(solution)/shard_map/concatenate | solution.py:94
  183.8 1.0 fusion.79
  184.8 0.3 bitcast_convert_fusion.2
  185.1 1.2 fusion.17
  186.3 1.2 fusion.12
  187.6 0.3 bitcast_convert_fusion
  187.9 1.2 fusion.7
  189.1 1.2 fusion.2
  190.4 5.1 %cosine_convert_fusion.2 = (bf16[128,2048]{1,0:T(8,128)(2,1)S(1)}, f32[128,2048]{1,0:T(8,128)S(1)}) fusion(f32[2048]{0:T(1024)S(1)} %multiply_multiply_fusion, f32[128]{0:T(128)S(1)} %multiply_multiply_fusion.1, f32[]{:T(128)} %bitcast.19, f32[129,2048]{1,0:T(8,128)S(1)} %fusion.2, f32[]{:T(128)S(6)} %div.123, f32[]{:T(128)S(6)} %sub.110, ...), kind=kLoop, calls=%fused_computation.104 | loop fusion | flops 7077888 | bytes 9970212 | tf_op jit(solution)/shard_map/convert.14
  195.5 13.9 %sine_convert_fusion.2 = (bf16[128,2048]{1,0:T(8,128)(2,1)S(1)}, bf16[128,2048]{1,0:T(8,128)(2,1)S(1)}, bf16[128,2048]{1,0:T(8,128)(2,1)S(1)}, bf16[128,2048]{1,0:T(8,128)(2,1)}, bf16[128,2048]{1,0:T(8,128)(2,1)S(1)}) fusion(f32[128,2048]{1,0:T(8,128)S(1)} %get-tuple-element.7, f32[2048]{0:T(1024)S(1)} %multiply_multiply_fusion, ...), kind=kLoop, calls=%fused_computation.103 | loop fusion | flops 3145728 | bytes 3678732 | tf_op jit(solution)/shard_map/convert.15
  209.4 0.4 convolution_convert_fusion.2
  209.9 0.1 fusion.80
  210.0 0.2 reshape.136
  210.2 0.2 reshape.137
  210.5 0.4 convolution_convert_fusion.1
  210.9 0.1 fusion.81
  211.0 0.2 reshape.138
  211.3 0.2 reshape.139
  211.5 1.5 convolution_convert_fusion
  213.0 0.9 fusion.82
  213.9 0.2 reshape.140
  214.1 1.3 reshape.141
  215.4 0.4 fusion.43
  215.9 0.4 fusion.50
  216.3 0.4 fusion.57
  216.7 3.1 %fusion.26 = f32[2048,128]{1,0:T(8,128)S(1)} fusion(f32[2048,256]{1,0:T(8,128)S(1)} %fusion.57, f32[2048,256]{1,0:T(8,128)S(1)} %fusion.50, f32[2048,256]{1,0:T(8,128)S(1)} %fusion.43, f32[]{:T(128)} %reduce_sum.9, f32[]{:T(128)} %bitcast.22, f32[]{:T(128)} %bitcast.20, f32[]{:T(128)} %bitcast), kind=kLoop, calls=%fused_computation.50 | loop fusion | flops 3932160 | bytes 7340048 | tf_op jit(solution)/shard_map/div | solution.py:85
  219.8 0.2 reshape.142
  220.0 0.9 multiply_convert_fusion
  (5 shorter events, 0.0 us)
Async XLA Ops:
  0.0 49.9 %copy-start = (s32[4,4,2]{1,2,0:T(2,128)S(1)}, s32[4,4,2]{1,2,0:T(2,128)}, u32[]{:S(2)}) copy-start(s32[4,4,2]{1,2,0:T(2,128)} %param.8) | copy-start | bytes 388
  1.3 70.6 %copy-start.1 = (f32[3]{0:T(128)S(1)}, f32[3]{0:T(128)}, u32[]{:S(2)}) copy-start(f32[3]{0:T(128)} %param.11) | copy-start | bytes 40
  1.3 71.9 %copy-start.2 = (f32[3]{0:T(128)S(1)}, f32[3]{0:T(128)}, u32[]{:S(2)}) copy-start(f32[3]{0:T(128)} %param.10) | copy-start | bytes 40
  1.3 72.6 %copy-start.3 = (s32[1,16]{1,0:T(1,128)S(1)}, s32[1,16]{1,0:T(1,128)}, u32[]{:S(2)}) copy-start(s32[1,16]{1,0:T(1,128)} %param.9) | copy-start | bytes 196
  37.0 57.8 %collective-permute-start = (bf16[4,128,2048]{2,1,0:T(8,128)(2,1)S(1)}, bf16[4,128,2048]{2,1,0:T(8,128)(2,1)}, u32[]{:S(2)}, u32[]{:S(2)}) collective-permute-start(bf16[4,128,2048]{2,1,0:T(8,128)(2,1)S(1)} %bitcast.32), channel_id=1, source_target_pairs={{0,508},{4,0},{8,4},{12,8},{16,12},{20,16},{24,20},{28,24},{32,28}... | collective-permute-start | bytes 6291464 | tf_op jit(solution)/shard_map/ppermute | solution.py:24
  46.8 133.7 %collective-permute-start.1 = (bf16[4,128,2048]{2,1,0:T(8,128)(2,1)S(1)}, bf16[4,128,2048]{2,1,0:T(8,128)(2,1)}, u32[]{:S(2)}, u32[]{:S(2)}) collective-permute-start(bf16[4,128,2048]{2,1,0:T(8,128)(2,1)S(1)} %bitcast.33), channel_id=1, source_target_pairs={{0,504},{4,508},{8,0},{12,4},{16,8},{20,12},{24,16},{28,20},{32,24... | collective-permute-start | bytes 6291464 | tf_op jit(solution)/shard_map/ppermute | solution.py:24
